TPU v7x, 128 devices: a whole 4x4x4 slice. The times are simulated.
128 devices in a mesh: prompt: 4 (over x), response: 16 (over y_lo, z, core), tensor: 2 (over y_hi).
Axes of the slice: x: 4, y: 4 (y_hi: 2, y_lo: 2; y = y_hi * 2 + y_lo), z: 4, core: 2. Of those that a mesh axis runs over, the one named last changes fastest.
Arguments:
- queries: bfloat16 [4, 2048, 8192], P('prompt', 'response', 'tensor'), may hold values from -30 to 30
- keys: bfloat16 [4, 2048, 1024], P('prompt', 'response', 'tensor'), may hold values from -6 to 6
- values: bfloat16 [4, 2048, 1024], P('prompt', 'response', 'tensor'), may hold values from -36 to 36
- prefix_keys: bfloat16 [4, 2048, 1024], P('prompt', ('response', 'tensor')), may hold values from -6 to 6
- prefix_values: bfloat16 [4, 2048, 1024], P('prompt', ('response', 'tensor')), may hold values from -36 to 36
- lengths: int32 [4, 16], P('prompt', 'response'), may hold values from 1 to 128, as said below
- out_grad: bfloat16 [4, 2048, 8192], P('prompt', 'response', 'tensor'), may hold values from -36 to 36
Outputs:
- output: bfloat16 [4, 2048, 8192], P('prompt', 'response', 'tensor')
- query_grad: bfloat16 [4, 2048, 8192], P('prompt', 'response', 'tensor')
- key_grad: bfloat16 [4, 2048, 1024], P('prompt', 'response', 'tensor')
- value_grad: bfloat16 [4, 2048, 1024], P('prompt', 'response', 'tensor')
- prefix_key_grad: bfloat16 [4, 2048, 1024], P('prompt', ('response', 'tensor'))
- prefix_value_grad: bfloat16 [4, 2048, 1024], P('prompt', ('response', 'tensor'))
Inputs may be any that keep to these rules, and one draw needn't show every extreme that they name: `lengths`: number of live tokens of response r of prompt p; they fill its first slots.
All inputs are finite; a program needn't handle non-finite values.
Results may differ from a plain program's by a relative error of at most 0.023.
Values may be sent and summed in bfloat16 or wider, within the bound.
A program may use at most 192 MiB of HBM per device.

v0:
```python
import math

import jax
import jax.numpy as jnp
from jax import lax
from jax.sharding import PartitionSpec as P

HD = 128
GROUP = 8


def attend_head(head_queries, own_keys, own_values, pre_keys, pre_values, live_rows, scaled_grad):
    row_count = head_queries.shape[0]
    prefix_len = pre_keys.shape[0]
    all_keys = jnp.concatenate([pre_keys, own_keys], axis=0)
    all_values = jnp.concatenate([pre_values, own_values], axis=0)
    factor = 1.0 / math.sqrt(head_queries.shape[2])
    scores = (
        jnp.einsum("rgd,kd->grk", head_queries, all_keys, preferred_element_type=jnp.float32)
        * factor
    )
    row_pos = jnp.arange(row_count, dtype=jnp.int32)[:, None]
    key_pos = jnp.arange(prefix_len + row_count, dtype=jnp.int32)[None, :] - prefix_len
    allowed = key_pos <= row_pos
    scores = jnp.where(allowed[None], scores, -1e30)
    row_max = jnp.max(scores, axis=2, keepdims=True)
    exponent = jnp.exp(scores - row_max)
    probs = exponent / jnp.sum(exponent, axis=2, keepdims=True)
    rounded = probs.astype(jnp.bfloat16)
    attended = jnp.einsum("grk,kd->rgd", rounded, all_values, preferred_element_type=jnp.float32)
    output = (attended * live_rows[:, None, None]).astype(jnp.bfloat16)
    grad_probs = jnp.einsum(
        "rgd,kd->grk", scaled_grad, all_values, preferred_element_type=jnp.float32
    )
    centre = jnp.sum(scaled_grad.astype(jnp.float32) * attended, axis=2)
    score_grad = (probs * (grad_probs - jnp.transpose(centre)[:, :, None]) * factor).astype(
        jnp.bfloat16
    )
    query_grad = jnp.einsum("grk,kd->rgd", score_grad, all_keys, preferred_element_type=jnp.float32)
    key_grad = jnp.einsum(
        "grk,rgd->kd", score_grad, head_queries, preferred_element_type=jnp.float32
    )
    value_grad = jnp.einsum("grk,rgd->kd", rounded, scaled_grad, preferred_element_type=jnp.float32)
    return (
        output,
        query_grad,
        key_grad[:prefix_len],
        key_grad[prefix_len:],
        value_grad[:prefix_len],
        value_grad[prefix_len:],
    )


def body(queries, keys, values, prefix_keys, prefix_values, lengths, out_grad):
    row_count = queries.shape[1]
    kv_cols = keys.shape[2]
    head_count = kv_cols // HD
    tensor_rank = lax.axis_index("tensor")
    full_keys, full_values = (
        lax.all_gather(prefix_keys, ("response", "tensor"), axis=1, tiled=True),
        lax.all_gather(prefix_values, ("response", "tensor"), axis=1, tiled=True),
    )
    pre_keys = lax.dynamic_slice_in_dim(full_keys, tensor_rank * kv_cols, kv_cols, 2)
    pre_values = lax.dynamic_slice_in_dim(full_values, tensor_rank * kv_cols, kv_cols, 2)
    length = lengths[0, 0]
    live_total = lax.psum(length.astype(jnp.float32), ("prompt", "response"))
    slots = row_count * lax.axis_size("prompt") * lax.axis_size("response")
    weight = slots / live_total
    live_rows = (jnp.arange(row_count, dtype=jnp.int32) < length).astype(jnp.float32)
    scaled = (out_grad[0].astype(jnp.float32) * live_rows[:, None] * weight).astype(jnp.bfloat16)
    outputs, query_grads, key_grads, value_grads, pre_kgs, pre_vgs = ([], [], [], [], [], [])
    for kv_head in range(head_count):
        qstart = kv_head * GROUP * HD
        kstart = kv_head * HD
        block_queries = queries[0, :, qstart : qstart + GROUP * HD].reshape(row_count, GROUP, HD)
        block_grad = scaled[:, qstart : qstart + GROUP * HD].reshape(row_count, GROUP, HD)
        results = attend_head(
            block_queries,
            keys[0, :, kstart : kstart + HD],
            values[0, :, kstart : kstart + HD],
            pre_keys[0, :, kstart : kstart + HD],
            pre_values[0, :, kstart : kstart + HD],
            live_rows,
            block_grad,
        )
        outputs.append(results[0].reshape(row_count, GROUP * HD))
        query_grads.append(results[1].reshape(row_count, GROUP * HD))
        pre_kgs.append(results[2])
        key_grads.append(results[3])
        pre_vgs.append(results[4])
        value_grads.append(results[5])
    output = jnp.concatenate(outputs, axis=1)[None]
    query_grad = jnp.concatenate(query_grads, axis=1).astype(jnp.bfloat16)[None]
    key_grad = jnp.concatenate(key_grads, axis=1).astype(jnp.bfloat16)[None]
    value_grad = jnp.concatenate(value_grads, axis=1).astype(jnp.bfloat16)[None]
    prefix_kterm = jnp.concatenate(pre_kgs, axis=1)[None]
    prefix_vterm = jnp.concatenate(pre_vgs, axis=1)[None]
    all_cols = kv_cols * lax.axis_size("tensor")
    empty = jnp.zeros((1, prefix_kterm.shape[1], all_cols), jnp.float32)
    placed_keys = lax.dynamic_update_slice_in_dim(empty, prefix_kterm, tensor_rank * kv_cols, 2)
    placed_values = lax.dynamic_update_slice_in_dim(empty, prefix_vterm, tensor_rank * kv_cols, 2)
    summed = (
        lax.psum_scatter(
            placed_keys.astype(jnp.bfloat16),
            ("response", "tensor"),
            scatter_dimension=1,
            tiled=True,
        ).astype(jnp.float32),
        lax.psum_scatter(
            placed_values.astype(jnp.bfloat16),
            ("response", "tensor"),
            scatter_dimension=1,
            tiled=True,
        ).astype(jnp.float32),
    )
    prefix_key_grad = summed[0].astype(jnp.bfloat16)
    prefix_value_grad = summed[1].astype(jnp.bfloat16)
    return (output, query_grad, key_grad, value_grad, prefix_key_grad, prefix_value_grad)


def solution(mesh):
    in_specs = (
        P("prompt", "response", "tensor"),
        P("prompt", "response", "tensor"),
        P("prompt", "response", "tensor"),
        P("prompt", ("response", "tensor"), None),
        P("prompt", ("response", "tensor"), None),
        P("prompt", "response"),
        P("prompt", "response", "tensor"),
    )
    out_specs = (
        P("prompt", "response", "tensor"),
        P("prompt", "response", "tensor"),
        P("prompt", "response", "tensor"),
        P("prompt", "response", "tensor"),
        P("prompt", ("response", "tensor"), None),
        P("prompt", ("response", "tensor"), None),
    )
    return jax.shard_map(body, mesh=mesh, in_specs=in_specs, out_specs=out_specs, check_vma=False)
```

profile of v0, /device:TPU:1, one launch (start us, length us, event | category | flops | bytes accessed | tf_op | source)
XLA Modules:
  0.0 577.8 jit_solution(16422370129197156738)
XLA Ops:
  9.4 141.8 %psum.7 = f32[]{:T(128)} all-reduce(f32[]{:T(128)S(6)} %convert_element_type.116), channel_id=1, replica_groups=mesh['prompt'=4,'response'=16,'tensor'=2] {'prompt','response'}, use_global_device_ids=true, to_apply=%region_8.9 | all-reduce | flops 1 | bytes 8 | tf_op jit(solution)/shard_map/psum | solution.py:66
  168.3 21.3 %all-gather.5.cloned.1.call-done = bf16[1,2048,1024]{2,1,0:T(8,128)(2,1)} async-done(((bf16[1,64,1024]{2,1,0:T(8,128)(2,1)}), bf16[1,2048,1024]{2,1,0:T(8,128)(2,1)}) %all-gather.5.cloned.1.call-update) | async-done | bytes 4194320 | tf_op jit(solution)/shard_map/all_gather | solution.py:60
  191.4 6.3 %fusion.93 = (f32[8,128]{1,0:T(8,128)S(1)}, f32[8,128,2176]{1,2,0:T(8,128)}) fusion(pred[128,2176]{0,1:T(8,128)(4,1)} %iota_compare_fusion, bf16[128,8,128]{0,2,1:T(8,128)(2,1)S(1)} %bitcast.296, bf16[128,128]{1,0:T(8,128)(2,1)S(1)} %get-tuple-element.54, bf16[2048,128]{1,0:T(8,128)(2,1)S(1)} %get-tuple-element.31), kind=kOutput, calls=%fused_computation.165 | convolution fusion | flops 580454528 | bytes 10014720 | tf_op jit(solution)/shard_map/sub | solution.py:27
  197.7 4.4 fusion.35
  210.0 6.3 %fusion.95 = (f32[8,128]{1,0:T(8,128)S(1)}, f32[8,128,2176]{1,2,0:T(8,128)}) fusion(pred[128,2176]{0,1:T(8,128)(4,1)} %iota_compare_fusion, bf16[128,8,128]{0,2,1:T(8,128)(2,1)S(1)} %bitcast.294, bf16[128,128]{1,0:T(8,128)(2,1)S(1)} %get-tuple-element.53, bf16[2048,128]{1,0:T(8,128)(2,1)S(1)} %get-tuple-element.30), kind=kOutput, calls=%fused_computation.167 | convolution fusion | flops 580454528 | bytes 10014720 | tf_op jit(solution)/shard_map/sub | solution.py:27
  216.3 4.4 fusion.33
  228.5 5.2 fusion.94
  233.8 4.4 fusion.34
  246.8 5.2 fusion.96
  252.0 4.4 fusion.32
  259.9 2.2 fusion.15
  265.3 2.8 copy.176
  268.1 2.6 broadcast_in_dim.41.clone
  272.2 3.8 convolution_bitcast_fusion
  276.1 4.0 convolution_bitcast_fusion.2
  280.2 3.9 convolution_bitcast_fusion.1
  287.6 2.5 copy.177
  290.2 2.6 broadcast_in_dim.41.clone.1
  294.4 3.2 convolution_convert_fusion
  298.6 3.1 convolution_convert_fusion.2
  304.4 3.3 convolution_convert_fusion.1
  314.4 3.3 convolution_convert_fusion.3
  320.1 101.5 %reduce-scatter.3.cloned.1.call-done = bf16[1,64,1024]{2,1,0:T(8,128)(2,1)} async-done(((bf16[1,2048,1024]{2,1,0:T(8,128)(2,1)}), bf16[1,64,1024]{2,1,0:T(8,128)(2,1)}) %reduce-scatter.3.cloned.1.call-update) | async-done | bytes 131088 | tf_op jit(solution)/shard_map/reduce_scatter | solution.py:103
  421.6 149.6 %reduce-scatter.5.cloned.1.call-done = bf16[1,64,1024]{2,1,0:T(8,128)(2,1)} async-done(((bf16[1,2048,1024]{2,1,0:T(8,128)(2,1)}), bf16[1,64,1024]{2,1,0:T(8,128)(2,1)}) %reduce-scatter.5.cloned.1.call-update) | async-done | bytes 131088 | tf_op jit(solution)/shard_map/reduce_scatter | solution.py:109
  (236 shorter events, 69.5 us)
Async XLA Ops:
  7.2 151.4 %copy-start.39 = (bf16[1,128,4096]{2,1,0:T(8,128)(2,1)S(1)}, bf16[1,128,4096]{2,1,0:T(8,128)(2,1)}, u32[]{:S(2)}) copy-start(bf16[1,128,4096]{2,1,0:T(8,128)(2,1)} %param.7) | copy-start | bytes 3145732
  7.2 155.3 %all-gather.3.cloned.1.call-start = ((), (), s32[]{:S(2)}) async-start(), calls=%async_computation.2 | async-start | bytes 4325376 | tf_op jit(solution)/shard_map/all_gather | solution.py:61
  7.9 181.7 %all-gather.5.cloned.1.call-start = ((), (), s32[]{:S(2)}) async-start(), calls=%async_computation.3 | async-start | bytes 4325376 | tf_op jit(solution)/shard_map/all_gather | solution.py:60
  8.7 412.9 %reduce-scatter.3.cloned.1.call-start = ((), (), s32[]{:S(2)}) async-start(), calls=%async_computation.4 | async-start | bytes 4325376 | tf_op jit(solution)/shard_map/reduce_scatter | solution.py:103
  157.5 46.2 %copy-start.29 = (bf16[128,1024]{0,1:T(8,128)(2,1)}, bf16[128,1024]{0,1:T(8,128)(2,1)S(1)}, u32[]{:S(2)}) copy-start(bf16[128,1024]{0,1:T(8,128)(2,1)S(1)} %copy.159) | copy-start | bytes 786436
  158.6 63.7 %copy-start.31 = (bf16[128,1024]{0,1:T(8,128)(2,1)}, bf16[128,1024]{0,1:T(8,128)(2,1)S(1)}, u32[]{:S(2)}) copy-start(bf16[128,1024]{0,1:T(8,128)(2,1)S(1)} %copy.149) | copy-start | bytes 786436
  160.5 49.4 %copy-start.35 = (bf16[1,128,1024]{1,2,0:T(8,128)(2,1)}, bf16[1,128,1024]{1,2,0:T(8,128)(2,1)S(1)}, u32[]{:S(2)}) copy-start(bf16[1,128,1024]{1,2,0:T(8,128)(2,1)S(1)} %copy.226) | copy-start | bytes 786436
  160.7 30.6 %copy-start.37 = (bf16[1,128,1024]{1,2,0:T(8,128)(2,1)}, bf16[1,128,1024]{1,2,0:T(8,128)(2,1)S(1)}, u32[]{:S(2)}) copy-start(bf16[1,128,1024]{1,2,0:T(8,128)(2,1)S(1)} %copy.232) | copy-start | bytes 786436
  160.8 30.6 %copy-start.54 = (bf16[128,128]{1,0:T(8,128)(2,1)}, bf16[128,128]{1,0:T(8,128)(2,1)S(1)}, u32[]{:S(2)}) copy-start(bf16[128,128]{1,0:T(8,128)(2,1)S(1)} %get-tuple-element.54) | copy-start | bytes 98308
  160.8 49.2 %copy-start.52 = (bf16[128,128]{1,0:T(8,128)(2,1)}, bf16[128,128]{1,0:T(8,128)(2,1)S(1)}, u32[]{:S(2)}) copy-start(bf16[128,128]{1,0:T(8,128)(2,1)S(1)} %get-tuple-element.53) | copy-start | bytes 98308
  191.3 18.7 %copy-start.23 = (bf16[2048,128]{1,0:T(8,128)(2,1)}, bf16[2048,128]{1,0:T(8,128)(2,1)S(1)}, u32[]{:S(2)}) copy-start(bf16[2048,128]{1,0:T(8,128)(2,1)S(1)} %get-tuple-element.30) | copy-start | bytes 1572868
  191.3 37.2 %copy-start.22 = (bf16[2048,128]{1,0:T(8,128)(2,1)}, bf16[2048,128]{1,0:T(8,128)(2,1)S(1)}, u32[]{:S(2)}) copy-start(bf16[2048,128]{1,0:T(8,128)(2,1)S(1)} %get-tuple-element.29) | copy-start | bytes 1572868
  191.3 55.5 %copy-start.21 = (bf16[2048,128]{1,0:T(8,128)(2,1)}, bf16[2048,128]{1,0:T(8,128)(2,1)S(1)}, u32[]{:S(2)}) copy-start(bf16[2048,128]{1,0:T(8,128)(2,1)S(1)} %get-tuple-element.28) | copy-start | bytes 1572868
  233.7 7.9 %slice-start.12 = ((s8[8912896]{0:T(1024)(128)(4,1)}), s8[4194304]{0:T(1024)(128)(4,1)S(1)}, s32[]{:S(2)}) async-start(s8[8912896]{0:T(1024)(128)(4,1)} %bitcast.280), calls=%async_computation.18 | async-start | bytes 8388608
  233.7 7.9 %slice-start.13 = ((s8[8912896]{0:T(1024)(128)(4,1)}), s8[524288]{0:T(1024)(128)(4,1)S(1)}, s32[]{:S(2)}) async-start(s8[8912896]{0:T(1024)(128)(4,1)} %bitcast.280), calls=%async_computation.19 | async-start | bytes 1048576
  252.0 7.9 %slice-start.4 = ((s8[8912896]{0:T(1024)(128)(4,1)}), s8[524288]{0:T(1024)(128)(4,1)S(1)}, s32[]{:S(2)}) async-start(s8[8912896]{0:T(1024)(128)(4,1)} %bitcast.274), calls=%async_computation.10 | async-start | bytes 1048576
  272.2 299.1 %reduce-scatter.5.cloned.1.call-start = ((), (), s32[]{:S(2)}) async-start(), calls=%async_computation.5 | async-start | bytes 4325376 | tf_op jit(solution)/shard_map/reduce_scatter | solution.py:109
  276.1 8.0 %copy-start.17 = (bf16[2176,128]{0,1:T(8,128)(2,1)}, bf16[2176,128]{0,1:T(8,128)(2,1)S(1)}, u32[]{:S(2)}) copy-start(bf16[2176,128]{0,1:T(8,128)(2,1)S(1)} %convolution_bitcast_fusion) | copy-start | bytes 1671172
  276.1 8.9 %slice-start = ((s8[4456448]{0:T(1024)(128)(4,1)}), s8[4194304]{0:T(1024)(128)(4,1)S(1)}, s32[]{:S(2)}) async-start(s8[4456448]{0:T(1024)(128)(4,1)} %bitcast.272), calls=%async_computation.6 | async-start | bytes 8388608
  301.7 8.7 %copy-start.18 = (bf16[2176,128]{0,1:T(8,128)(2,1)S(1)}, bf16[2176,128]{0,1:T(8,128)(2,1)}, u32[]{:S(2)}) copy-start(bf16[2176,128]{0,1:T(8,128)(2,1)} %copy-done.17) | copy-start | bytes 1671172
  301.7 11.0 %copy-start.11 = (bf16[2176,128]{0,1:T(8,128)(2,1)S(1)}, bf16[2176,128]{0,1:T(8,128)(2,1)}, u32[]{:S(2)}) copy-start(bf16[2176,128]{0,1:T(8,128)(2,1)} %copy-done.10) | copy-start | bytes 1671172
  301.7 11.0 %copy-start.15 = (bf16[2176,128]{0,1:T(8,128)(2,1)S(1)}, bf16[2176,128]{0,1:T(8,128)(2,1)}, u32[]{:S(2)}) copy-start(bf16[2176,128]{0,1:T(8,128)(2,1)} %copy-done.14) | copy-start | bytes 1671172
  301.7 11.0 %copy-start.13 = (bf16[2176,128]{0,1:T(8,128)(2,1)S(1)}, bf16[2176,128]{0,1:T(8,128)(2,1)}, u32[]{:S(2)}) copy-start(bf16[2176,128]{0,1:T(8,128)(2,1)} %copy-done.12) | copy-start | bytes 1671172
  308.5 9.4 %copy-start.40 = (bf16[1,128,1024]{2,1,0:T(8,128)(2,1)S(1)}, bf16[1,128,1024]{2,1,0:T(8,128)(2,1)}, u32[]{:S(2)}) copy-start(bf16[1,128,1024]{2,1,0:T(8,128)(2,1)} %copy.167) | copy-start | bytes 786436
  (59 other events, 246.5 us)
Sparse Core Ops, SparseCore 0:
  9.7 90.2 all-gather.2
  101.7 87.8 all-gather.4
  272.3 149.2 reduce-scatter.2
  424.4 146.7 reduce-scatter.4
where the time goes:
time: 581 us; the launch traced here: 578 us
  waiting for transfers between devices  274 us (47%)
  blocking collectives  142 us (24%)
  matrix products  70.2 us (12%)
  local copies, waits for them, and re-layouts  52.3 us (9%)
  other arithmetic  23.4 us (4%)
  between operations  16.2 us (3%)
    reduce_scatter x1, waiting for transfers between devices, body(): lax.psum_scatter(placed_values.astype(jnp.bfloat16), ('response', 'tensor...  150 us
    psum x1, blocking collectives, body(): live_total = lax.psum(length.astype(jnp.float32), ('prompt', 'response'))  142 us
    reduce_scatter x1, waiting for transfers between devices, body(): lax.psum_scatter(placed_keys.astype(jnp.bfloat16), ('response', 'tensor')...  102 us
    unnamed x164, local copies, waits for them, and re-layouts  23.7 us
    sub x4, matrix products, attend_head(): exponent = jnp.exp(scores - row_max)  23 us
    all_gather x1, waiting for transfers between devices, body(): lax.all_gather(prefix_keys, ('response', 'tensor'), axis=1, tiled=True)  21.3 us
    convert_element_type x4, other arithmetic, attend_head(): rounded = probs.astype(jnp.bfloat16)  17.7 us
    dot_general x4, matrix products, attend_head(): jnp.einsum('grk,rgd->kd', rounded, scaled_grad, preferred_element_type=jn...  13.3 us
  transfers between devices with their start and end apart: 4, of which 3 were waited for; matrix products, arithmetic and copies ran while one was open for 11% of the time, Pallas kernels for 0%

commit v1 on v0

v1 whole, which is shorter than its diff:
```python
import math

import jax
import jax.numpy as jnp
from jax import lax
from jax.experimental import pallas as pl
from jax.experimental.pallas import tpu as pltpu
from jax.sharding import PartitionSpec as P

HD = 128
GROUP = 8
ROWS = 128
LOCAL = 64
BLOCK = 512
NBLOCK = 4
CHUNK = 1024
HALF = 512
HEADS = 2
QCOLS = HEADS * GROUP * HD
KCOLS = HEADS * HD
FACTOR = 1.0 / math.sqrt(HD)
EXP2 = math.log2(math.e) * FACTOR
MESH = pl.DeviceIdType.MESH
f32 = jnp.float32
bf16 = jnp.bfloat16


def dot(a, b):
    return jnp.dot(a, b, preferred_element_type=f32)


def kernel(
    q_in, k_in, v_in, pk_in, pv_in, len_in, do_in,
    o_out, dq_out, dk_out, dv_out, pkg_out, pvg_out,
    pk, pv, qin, din, kown, vown, kbuf, vbuf, lens, lsum,
    qt, qn, dot_, don, vt, kt, kot, vot, e, eo, mx, acc, cen, dq,
    ost, dqst, dkst, dvst, dks, dvs, rk, rv,
    load_sem, pair_send, pair_recv, own_sem, k_send, v_send, k_recv, v_recv,
    len_send, len_recv, dk_send, dv_send, dk_recv, dv_recv, out_send, out_recv, out_sem,
):
    prompt = lax.axis_index("prompt")
    resp = lax.axis_index("response")
    y_hi = lax.axis_index("tensor")
    core = lax.rem(resp, 2)
    z = lax.rem(resp // 2, 4)
    y_lo = resp // 8
    y = y_hi * 2 + y_lo
    other = 1 - core

    def at(zz, yy, cc):
        return {"response": lax.rem(yy, 2) * 8 + zz * 2 + cc, "tensor": yy // 2}

    def along_x(pp):
        return {"prompt": pp}

    sibling = {"response": resp + 1 - 2 * core}
    my_q = pl.ds(pl.multiple_of(core * QCOLS, QCOLS), QCOLS)
    its_q = pl.ds(pl.multiple_of(other * QCOLS, QCOLS), QCOLS)
    my_k = pl.ds(pl.multiple_of(core * KCOLS, KCOLS), KCOLS)
    its_k = pl.ds(pl.multiple_of(other * KCOLS, KCOLS), KCOLS)

    loads = [
        pltpu.make_async_copy(pk_in.at[0], pk, load_sem.at[0]),
        pltpu.make_async_copy(pv_in.at[0], pv, load_sem.at[1]),
        pltpu.make_async_copy(q_in.at[0, :, my_q], qin.at[0], load_sem.at[2]),
        pltpu.make_async_copy(do_in.at[0, :, my_q], din.at[0], load_sem.at[3]),
        pltpu.make_async_copy(k_in.at[0, :, my_k], kown.at[0], load_sem.at[4]),
        pltpu.make_async_copy(v_in.at[0, :, my_k], vown.at[0], load_sem.at[5]),
    ]
    for copy in loads:
        copy.start()

    barrier = pltpu.get_barrier_semaphore()

    @pl.loop(1, 32)
    def _(j):
        pl.semaphore_signal(
            barrier,
            inc=1,
            device_id=at(
                lax.rem(z + j // 8, 4),
                lax.rem(y + lax.rem(j // 2, 4), 4),
                lax.rem(core + lax.rem(j, 2), 2),
            ),
            device_id_type=MESH,
        )

    for step in range(1, 4):
        pl.semaphore_signal(
            barrier, inc=1, device_id=along_x(lax.rem(prompt + step, 4)), device_id_type=MESH
        )
    pl.semaphore_wait(barrier, 34)

    def send(src, dst, send_sem, recv_sem, device):
        return pltpu.make_async_remote_copy(
            src_ref=src,
            dst_ref=dst,
            send_sem=send_sem,
            recv_sem=recv_sem,
            device_id=device,
            device_id_type=MESH,
        )

    lens[0, prompt] = jnp.full((8, 128), len_in[0, 0], jnp.int32).astype(f32)
    pair = [
        send(lens.at[0, prompt], lsum.at[1], pair_send.at[0], pair_recv.at[0], sibling),
        send(q_in.at[0, :, its_q], qin.at[1], pair_send.at[1], pair_recv.at[1], sibling),
        send(k_in.at[0, :, its_k], kown.at[1], pair_send.at[2], pair_recv.at[2], sibling),
        send(do_in.at[0, :, its_q], din.at[1], pair_send.at[3], pair_recv.at[3], sibling),
        send(v_in.at[0, :, its_k], vown.at[1], pair_send.at[4], pair_recv.at[4], sibling),
    ]
    lsum[0] = lens[0, prompt]
    pair[0].start()
    pair[1].start()
    pair[2].start()

    my_row = pl.multiple_of((y * 2 + core) * LOCAL, LOCAL)
    order = ((0, 0), (1, 1), (2, 3), (3, 2))

    def push(shard, buf, send_sems, recv_sems):
        for block, dist in order:
            to_z = lax.rem(z + 4 - dist, 4)
            for n in range(8):
                if block == 0 and n == 0:
                    continue
                to_y = lax.rem(y + n // 2, 4)
                to_core = lax.rem(core + n % 2, 2)
                cols = pl.multiple_of(((to_y // 2) * 2 + to_core) * KCOLS, KCOLS)
                send(
                    shard.at[:, pl.ds(cols, KCOLS)],
                    buf.at[pl.ds(block * BLOCK + my_row, LOCAL)],
                    send_sems.at[block * 8 + n],
                    recv_sems.at[block],
                    at(to_z, to_y, to_core),
                ).start()

    def push_done(shard, buf, send_sems, recv_sems):
        @pl.loop(1, 32)
        def _(n):
            send(
                shard.at[:, pl.ds(0, KCOLS)],
                buf.at[pl.ds(0, LOCAL)],
                send_sems.at[n],
                recv_sems.at[0],
                sibling,
            ).wait_send()

    mine = pl.ds(pl.multiple_of((y_hi * 2 + core) * KCOLS, KCOLS), KCOLS)
    loads[0].wait()
    push(pk, kbuf, k_send, k_recv)
    pltpu.make_async_copy(pk.at[:, mine], kbuf.at[pl.ds(my_row, LOCAL)], k_recv.at[0]).start()
    pair[3].start()
    pair[4].start()
    loads[1].wait()
    push(pv, vbuf, v_send, v_recv)
    pltpu.make_async_copy(pv.at[:, mine], vbuf.at[pl.ds(my_row, LOCAL)], v_recv.at[0]).start()

    def x_copy(step):
        return send(
            lens.at[0, prompt], lens.at[0, prompt], len_send.at[0, step - 1],
            len_recv.at[0, step - 1], along_x(lax.rem(prompt + step, 4)),
        )

    def z_copy(step):
        return send(
            lens.at[1, z], lens.at[1, z], len_send.at[1, step - 1],
            len_recv.at[1, step - 1], at(lax.rem(z + step, 4), y, core),
        )

    rest = y_lo * 2 + core

    def rest_copy(step):
        slot = lax.rem(rest + step, 4)
        return send(
            lens.at[2, rest], lens.at[2, rest], len_send.at[2, step - 1],
            len_recv.at[2, step - 1], at(z, y_hi * 2 + slot // 2, lax.rem(slot, 2)),
        )

    for step in range(1, 4):
        x_copy(step).start()

    slot_row = lax.broadcasted_iota(jnp.int32, (ROWS, HD), 0).astype(f32)

    def stage_q(s):
        for h in range(HEADS):
            for g in range(GROUP):
                cols = pl.ds((h * GROUP + g) * HD, HD)
                block = qin[s, :, cols]
                qn[h, s, g * ROWS : (g + 1) * ROWS, :] = block
                qt[h, s, :, g * ROWS : (g + 1) * ROWS] = block.T

    def stage_do(s):
        live = slot_row < lsum[s, 0:1, :]
        for h in range(HEADS):
            for g in range(GROUP):
                cols = pl.ds((h * GROUP + g) * HD, HD)
                block = jnp.where(live, din[s, :, cols].astype(f32), 0.0).astype(bf16)
                dot_[h, s, :, g * ROWS : (g + 1) * ROWS] = block.T

    def stage_own(s):
        for h in range(HEADS):
            cols = pl.ds(h * HD, HD)
            kot[h, s] = kown[s, :, cols].T
            vot[h, s, 0:HD] = vown[s, :, cols].T
            vot[h, s, HD : HD + 16] = jnp.ones((16, ROWS), bf16)

    allowed = lax.broadcasted_iota(jnp.int32, (ROWS, HALF), 0) <= lax.rem(
        lax.broadcasted_iota(jnp.int32, (ROWS, HALF), 1), ROWS
    )

    def own_scores(h, s, part):
        scores = dot(kown[s, :, pl.ds(h * HD, HD)], qt[h, s, :, part * HALF : (part + 1) * HALF])
        return jnp.where(allowed, scores, -1e30)

    def own_max(s):
        for h in range(HEADS):
            for part in range(2):
                cols = pl.ds(part * HALF, HALF)
                mx[h, s, :, cols] = jnp.max(
                    own_scores(h, s, part).reshape(ROWS // 8, 8, HALF), axis=0
                )

    loads[2].wait()
    loads[4].wait()
    stage_q(0)
    own_max(0)
    loads[3].wait()
    stage_do(0)
    loads[5].wait()
    stage_own(0)
    for h in range(HEADS):
        vt[h, HD : HD + 16] = jnp.ones((16, NBLOCK * BLOCK), bf16)
    pair[0].wait_recv()
    pair[1].wait_recv()
    pair[2].wait_recv()
    stage_q(1)
    own_max(1)

    @pl.loop(0, NBLOCK)
    def _(j):
        base = pl.multiple_of(j * BLOCK, BLOCK)
        keys = kbuf.at[pl.ds(base, BLOCK)]
        pltpu.make_async_copy(keys, keys, k_recv.at[j]).wait()
        for h in range(HEADS):
            cols = pl.ds(h * HD, HD)
            for n in range(BLOCK // 128):
                kt[h, :, pl.ds(base + n * 128, 128)] = kbuf[pl.ds(base + n * 128, 128), cols].T
            for s in range(2):
                for part in range(2):
                    rows = pl.ds(part * HALF, HALF)
                    scores = dot(kbuf[pl.ds(base, BLOCK), cols], qt[h, s, :, rows])
                    mx[h, s, :, rows] = jnp.maximum(
                        mx[h, s, :, rows],
                        jnp.max(scores.reshape(BLOCK // 8, 8, HALF), axis=0),
                    )

    for step in range(1, 4):
        x_copy(step).wait_recv()
    lens[1, z] = lens[0, 0] + lens[0, 1] + lens[0, 2] + lens[0, 3]
    for step in range(1, 4):
        z_copy(step).start()

    pair[3].wait_recv()
    pair[4].wait_recv()
    stage_do(1)
    stage_own(1)

    for h in range(HEADS):
        for s in range(2):
            top = jnp.max(mx[h, s], axis=0, keepdims=True) * EXP2
            mx[h, s] = jnp.broadcast_to(top, (8, CHUNK))
            for part in range(2):
                rows = pl.ds(part * HALF, HALF)
                power = jnp.exp2(own_scores(h, s, part) * EXP2 - mx[h, s, 0:1, rows]).astype(bf16)
                eo[h, s, :, rows] = power
                acc[h, s, :, rows] = dot(vot[h, s], power)

    @pl.loop(0, NBLOCK)
    def _(j):
        base = pl.multiple_of(j * BLOCK, BLOCK)
        vals = vbuf.at[pl.ds(base, BLOCK)]
        pltpu.make_async_copy(vals, vals, v_recv.at[j]).wait()
        for h in range(HEADS):
            cols = pl.ds(h * HD, HD)
            for n in range(BLOCK // 128):
                vt[h, 0:HD, pl.ds(base + n * 128, 128)] = vbuf[
                    pl.ds(base + n * 128, 128), cols
                ].T
            for s in range(2):
                for part in range(2):
                    rows = pl.ds(part * HALF, HALF)
                    scores = dot(kbuf[pl.ds(base, BLOCK), cols], qt[h, s, :, rows])
                    power = jnp.exp2(scores * EXP2 - mx[h, s, 0:1, rows]).astype(bf16)
                    e[h, j, s, :, rows] = power
                    acc[h, s, :, rows] += dot(vt[h, :, pl.ds(base, BLOCK)], power)

    for step in range(1, 4):
        z_copy(step).wait_recv()
    lens[2, rest] = lens[1, 0] + lens[1, 1] + lens[1, 2] + lens[1, 3]
    for step in range(1, 4):
        rest_copy(step).start()

    def put(src, out, dst_cols, n):
        return (
            pltpu.make_async_copy(src.at[0], out.at[0, :, dst_cols], out_sem.at[n]),
            send(src.at[1], out.at[0, :, dst_cols], out_send.at[n], out_recv.at[n], sibling),
        )

    for s in range(2):
        live = slot_row < lsum[s, 0:1, :]
        for h in range(HEADS):
            inv = 1.0 / acc[h, s, HD : HD + 1, :]
            attended = acc[h, s, 0:HD, :] * inv
            cotangent = dot_[h, s].astype(f32)
            cen[h, s] = jnp.sum(attended * cotangent, axis=0, keepdims=True) * inv
            scaled = (cotangent * inv).astype(bf16)
            dot_[h, s] = scaled
            for g in range(GROUP):
                rows = slice(g * ROWS, (g + 1) * ROWS)
                don[h, s, rows, :] = scaled[:, rows].T
                ost[s, :, pl.ds((h * GROUP + g) * HD, HD)] = jnp.where(
                    live, attended[:, rows].T, 0.0
                ).astype(bf16)
    o_copies = put(ost, o_out, my_q, 0)
    o_copies[0].start()
    o_copies[1].start()

    for step in range(1, 4):
        rest_copy(step).wait_recv()
    total = lens[2, 0] + lens[2, 1] + lens[2, 2] + lens[2, 3]
    weight = (4.0 * 16.0 * ROWS) / total[0:1, :]

    for h in range(HEADS):
        cols = pl.ds(h * HD, HD)
        for s in range(2):
            power = eo[h, s]
            grad = dot(vown[s, :, cols], dot_[h, s])
            score = (power.astype(f32) * (grad - cen[h, s])).astype(bf16)
            dvst[s, :, cols] = (dot(power, don[h, s]) * weight).astype(bf16)
            dkst[s, :, cols] = (dot(score, qn[h, s]) * (weight * FACTOR)).astype(bf16)
            dq[h, s] = dot(kot[h, s], score)
    dk_copies = put(dkst, dk_out, my_k, 1)
    dv_copies = put(dvst, dv_out, my_k, 2)
    for copy in dk_copies + dv_copies:
        copy.start()

    slot = (y_hi * 2 + core) * 8 + z * 2 + y_lo

    def grad_copy(j, n, stage, landing, send_sems, recv_sem):
        dist = j + (j // 2) * (5 - 2 * j)
        row = pl.multiple_of(j * BLOCK + n * LOCAL, LOCAL)
        return send(
            stage.at[pl.ds(row, LOCAL)],
            landing.at[slot],
            send_sems.at[j * 8 + n],
            recv_sem,
            at(lax.rem(z + dist, 4), n // 2, lax.rem(n, 2)),
        )

    def self_copy(stage, landing, recv_sem):
        return pltpu.make_async_copy(stage.at[pl.ds(my_row, LOCAL)], landing.at[slot], recv_sem)

    me = y * 2 + core

    @pl.loop(0, NBLOCK)
    def _(back):
        j = NBLOCK - 1 - back
        base = pl.multiple_of(j * BLOCK, BLOCK)
        for h in range(HEADS):
            cols = pl.ds(h * HD, HD)
            dv_part = None
            dk_part = None
            for s in range(2):
                power = e[h, j, s]
                grad = dot(vbuf[pl.ds(base, BLOCK), cols], dot_[h, s])
                score = (power.astype(f32) * (grad - cen[h, s])).astype(bf16)
                dv_now = dot(power, don[h, s])
                dk_now = dot(score, qn[h, s])
                dv_part = dv_now if s == 0 else dv_part + dv_now
                dk_part = dk_now if s == 0 else dk_part + dk_now
                dq[h, s] += dot(kt[h, :, pl.ds(base, BLOCK)], score)
            dvs[pl.ds(base, BLOCK), cols] = dv_part.astype(bf16)
            dks[pl.ds(base, BLOCK), cols] = dk_part.astype(bf16)

        @pl.loop(0, 8)
        def _(n):
            @pl.when(jnp.logical_or(j > 0, n != me))
            def _():
                grad_copy(j, n, dvs, rv, dv_send, dv_recv).start()
                grad_copy(j, n, dks, rk, dk_send, dk_recv).start()

    self_copy(dvs, rv, dv_recv).start()
    self_copy(dks, rk, dk_recv).start()

    for s in range(2):
        for h in range(HEADS):
            for g in range(GROUP):
                rows = slice(g * ROWS, (g + 1) * ROWS)
                dqst[s, :, pl.ds((h * GROUP + g) * HD, HD)] = (
                    dq[h, s, :, rows].T * (weight * FACTOR)
                ).astype(bf16)
    dq_copies = put(dqst, dq_out, my_q, 3)
    for copy in dq_copies:
        copy.start()

    wide = jnp.concatenate([weight, weight], axis=1)
    pltpu.make_async_copy(rv, rv, dv_recv).wait()
    for n in range(4):
        total_v = rv[n * 8].astype(f32)
        for m in range(1, 8):
            total_v += rv[n * 8 + m].astype(f32)
        pvg_out[0, :, n * KCOLS : (n + 1) * KCOLS] = (total_v * wide).astype(bf16)
    pltpu.make_async_copy(rk, rk, dk_recv).wait()
    for n in range(4):
        total_k = rk[n * 8].astype(f32)
        for m in range(1, 8):
            total_k += rk[n * 8 + m].astype(f32)
        pkg_out[0, :, n * KCOLS : (n + 1) * KCOLS] = (total_k * (wide * FACTOR)).astype(bf16)

    push_done(pk, kbuf, k_send, k_recv)
    push_done(pv, vbuf, v_send, v_recv)
    for copy in pair:
        copy.wait_send()
    for step in range(1, 4):
        x_copy(step).wait_send()
        z_copy(step).wait_send()
        rest_copy(step).wait_send()

    @pl.loop(0, 32)
    def _(n):
        @pl.when(n != me)
        def _():
            grad_copy(n // 8, lax.rem(n, 8), dvs, rv, dv_send, dv_recv).wait_send()
            grad_copy(n // 8, lax.rem(n, 8), dks, rk, dk_send, dk_recv).wait_send()

    for local, remote in (o_copies, dk_copies, dv_copies, dq_copies):
        local.wait()
        remote.wait_send()
        remote.wait_recv()


def body(queries, keys, values, prefix_keys, prefix_values, lengths, out_grad):
    vmem = lambda shape, dtype: pltpu.VMEM(shape, dtype)
    dma = pltpu.SemaphoreType.DMA
    prefix = NBLOCK * BLOCK
    anywhere = pl.BlockSpec(memory_space=pl.ANY)
    in_vmem = pl.BlockSpec(memory_space=pltpu.VMEM)
    shape = lambda a: jax.ShapeDtypeStruct(a.shape, bf16)
    return pl.pallas_call(
        kernel,
        out_shape=[
            shape(queries), shape(queries), shape(keys), shape(values),
            shape(prefix_keys), shape(prefix_values),
        ],
        in_specs=[anywhere] * 5 + [pl.BlockSpec(memory_space=pltpu.SMEM), anywhere],
        out_specs=[anywhere] * 4 + [in_vmem] * 2,
        scratch_shapes=[
            vmem((LOCAL, 8 * HD), bf16), vmem((LOCAL, 8 * HD), bf16),
            vmem((2, ROWS, QCOLS), bf16), vmem((2, ROWS, QCOLS), bf16),
            vmem((2, ROWS, KCOLS), bf16), vmem((2, ROWS, KCOLS), bf16),
            vmem((prefix, KCOLS), bf16), vmem((prefix, KCOLS), bf16),
            vmem((3, 4, 8, 128), f32), vmem((2, 8, 128), f32),
            vmem((HEADS, 2, HD, CHUNK), bf16), vmem((HEADS, 2, CHUNK, HD), bf16),
            vmem((HEADS, 2, HD, CHUNK), bf16), vmem((HEADS, 2, CHUNK, HD), bf16),
            vmem((HEADS, HD + 16, prefix), bf16), vmem((HEADS, HD, prefix), bf16),
            vmem((HEADS, 2, HD, ROWS), bf16), vmem((HEADS, 2, HD + 16, ROWS), bf16),
            vmem((HEADS, NBLOCK, 2, BLOCK, CHUNK), bf16),
            vmem((HEADS, 2, ROWS, CHUNK), bf16),
            vmem((HEADS, 2, 8, CHUNK), f32),
            vmem((HEADS, 2, HD + 16, CHUNK), f32),
            vmem((HEADS, 2, 1, CHUNK), f32),
            vmem((HEADS, 2, HD, CHUNK), f32),
            vmem((2, ROWS, QCOLS), bf16), vmem((2, ROWS, QCOLS), bf16),
            vmem((2, ROWS, KCOLS), bf16), vmem((2, ROWS, KCOLS), bf16),
            vmem((prefix, KCOLS), bf16), vmem((prefix, KCOLS), bf16),
            vmem((32, LOCAL, KCOLS), bf16), vmem((32, LOCAL, KCOLS), bf16),
            dma((6,)), dma((5,)), dma((5,)), dma((1,)),
            dma((32,)), dma((32,)), dma((NBLOCK,)), dma((NBLOCK,)),
            dma((3, 3)), dma((3, 3)),
            dma((32,)), dma((32,)), dma, dma,
            dma((4,)), dma((4,)), dma((4,)),
        ],
        compiler_params=pltpu.CompilerParams(
            collective_id=0, has_side_effects=True, vmem_limit_bytes=60 * 2**20
        ),
        cost_estimate=pl.CostEstimate(
            flops=14 * 2**30, bytes_accessed=10 * 2**20, transcendentals=9 * 2**20
        ),
    )(queries, keys, values, prefix_keys, prefix_values, lengths, out_grad)


def solution(mesh):
    in_specs = (
        P("prompt", "response", "tensor"),
        P("prompt", "response", "tensor"),
        P("prompt", "response", "tensor"),
        P("prompt", ("response", "tensor"), None),
        P("prompt", ("response", "tensor"), None),
        P("prompt", "response"),
        P("prompt", "response", "tensor"),
    )
    out_specs = (
        P("prompt", "response", "tensor"),
        P("prompt", "response", "tensor"),
        P("prompt", "response", "tensor"),
        P("prompt", "response", "tensor"),
        P("prompt", ("response", "tensor"), None),
        P("prompt", ("response", "tensor"), None),
    )
    return jax.shard_map(body, mesh=mesh, in_specs=in_specs, out_specs=out_specs, check_vma=False)
```

time: 581 us -> 90.7 us (0.16)
  waiting for transfers between devices: 274 us -> 0 us
  blocking collectives: 142 us -> 0 us
  Pallas kernels: 0 us -> 81.7 us
  matrix products: 70.2 us -> 0 us
  local copies, waits for them, and re-layouts: 52.3 us -> 6.91 us
  other arithmetic: 23.4 us -> 0 us
  between operations: 16.2 us -> 1.3 us
    reduce_scatter x2 -> x0, waiting for transfers between devices: 251 us -> none  [the longest x1 150 us: body(): lax.psum_scatter(placed_values.astype(jnp.bfloat16), ('response', 'tensor...]
    psum x1 -> x0, blocking collectives: 142 us -> none  [body(): live_total = lax.psum(length.astype(jnp.float32), ('prompt', 'response'))]
    pallas_call x0 -> x1, Pallas kernels: none -> 81.7 us  [body(): pl.pallas_call(kernel, out_shape=[shape(queries), shape(queries), shape(k...]
    dot_general x20 -> x0, matrix products: 47.2 us -> none  [the longest x4 13.3 us: attend_head(): jnp.einsum('grk,rgd->kd', rounded, scaled_grad, preferred_element_type=jn...]
    sub x4 -> x0, matrix products: 23 us -> none  [attend_head(): exponent = jnp.exp(scores - row_max)]
    all_gather x2 -> x0, waiting for transfers between devices: 21.3 us -> none  [the longest x1 21.3 us: body(): lax.all_gather(prefix_keys, ('response', 'tensor'), axis=1, tiled=True)]
    convert_element_type x6 -> x0, other arithmetic: 19.2 us -> none  [the longest x4 17.7 us: attend_head(): rounded = probs.astype(jnp.bfloat16)]
    unnamed x164 -> x16, local copies, waits for them, and re-layouts: 23.7 us -> 6.91 us
  transfers between devices with their start and end apart: 4 -> 0, of which waited for: 3 -> 0; matrix products, arithmetic and copies ran while one was open for 11% -> 0% of each run, Pallas kernels for 0% -> 0%
where the time goes in v1:
time: 90.7 us; the launch traced here: 89.9 us
  Pallas kernels  81.7 us (90%)
  local copies, waits for them, and re-layouts  6.91 us (8%)
  between operations  1.3 us (1%)
    pallas_call x1, Pallas kernels, body(): pl.pallas_call(kernel, out_shape=[shape(queries), shape(queries), shape(k...  81.7 us
    unnamed x16, local copies, waits for them, and re-layouts  6.91 us

profile of v1, /device:TPU:1, one launch (start us, length us, event | category | flops | bytes accessed | tf_op | source)
XLA Modules:
  0.0 89.9 jit_solution(10601072376141951757)
XLA Ops:
  1.3 81.7 %shard_map.118 = (bf16[1,128,4096]{2,1,0:T(8,128)(2,1)}, bf16[1,128,4096]{2,1,0:T(8,128)(2,1)}, bf16[1,128,512]{2,1,0:T(8,128)(2,1)}, bf16[1,128,512]{2,1,0:T(8,...) custom-call(bf16[1,128,4096]{2,1,0:T(8,128)(2,1)} %q_in.1, bf16[1,128,512]{2,1,0:T(8,128)(2,1)} %k_in.1, ...), custom_call_target="tpu_custom_call" | custom-call | flops 15032385536 | bytes 10485760 | tf_op jit(solution)/shard_map/pallas_call | solution.py:449
  83.0 0.0 copy-start
  83.0 2.4 %copy.20 = bf16[1,128,4096]{2,1,0:T(8,128)(2,1)} copy(bf16[1,128,4096]{2,1,0:T(8,128)(2,1)} %get-tuple-element.12) | data formatting | bytes 2097152
  85.4 0.0 copy-done
  85.4 0.0 copy-start.4
  85.4 1.0 %copy.21 = bf16[1,128,4096]{2,1,0:T(8,128)(2,1)} copy(bf16[1,128,4096]{2,1,0:T(8,128)(2,1)S(1)} %copy-done) | data formatting | bytes 2097152
  86.3 0.1 copy-done.4
  86.4 0.0 copy-start.3
  86.4 0.7 copy.22
  87.0 0.3 copy-done.3
  87.3 0.0 copy-start.2
  87.3 0.7 copy.23
  88.0 0.3 copy-done.2
  88.3 0.0 copy-start.1
  88.3 0.7 copy.24
  88.9 0.3 copy-done.1
  89.2 0.7 copy.25
Async XLA Ops:
  83.0 2.4 %copy-start = (bf16[1,128,4096]{2,1,0:T(8,128)(2,1)S(1)}, bf16[1,128,4096]{2,1,0:T(8,128)(2,1)}, u32[]{:S(2)}) copy-start(bf16[1,128,4096]{2,1,0:T(8,128)(2,1)} %get-tuple-element.13) | copy-start | bytes 3145732
  85.4 1.0 %copy-start.4 = (bf16[1,128,512]{2,1,0:T(8,128)(2,1)S(1)}, bf16[1,128,512]{2,1,0:T(8,128)(2,1)}, u32[]{:S(2)}) copy-start(bf16[1,128,512]{2,1,0:T(8,128)(2,1)} %get-tuple-element.14) | copy-start | bytes 393220
  86.4 1.0 %copy-start.3 = (bf16[1,128,512]{2,1,0:T(8,128)(2,1)S(1)}, bf16[1,128,512]{2,1,0:T(8,128)(2,1)}, u32[]{:S(2)}) copy-start(bf16[1,128,512]{2,1,0:T(8,128)(2,1)} %get-tuple-element.15) | copy-start | bytes 393220
  87.3 1.0 %copy-start.2 = (bf16[1,64,1024]{2,1,0:T(8,128)(2,1)S(1)}, bf16[1,64,1024]{2,1,0:T(8,128)(2,1)}, u32[]{:S(2)}) copy-start(bf16[1,64,1024]{2,1,0:T(8,128)(2,1)} %get-tuple-element.16) | copy-start | bytes 393220
  88.3 1.0 %copy-start.1 = (bf16[1,64,1024]{2,1,0:T(8,128)(2,1)S(1)}, bf16[1,64,1024]{2,1,0:T(8,128)(2,1)}, u32[]{:S(2)}) copy-start(bf16[1,64,1024]{2,1,0:T(8,128)(2,1)} %get-tuple-element.17) | copy-start | bytes 393220

commit v2 on v1

--- a/solution.py
+++ b/solution.py
@@ -34,9 +34,9 @@
     o_out, dq_out, dk_out, dv_out, pkg_out, pvg_out,
     pk, pv, qin, din, kown, vown, kbuf, vbuf, lens, lsum,
     qt, qn, dot_, don, vt, kt, kot, vot, e, eo, mx, acc, cen, dq,
-    ost, dqst, dkst, dvst, dks, dvs, rk, rv,
-    load_sem, pair_send, pair_recv, own_sem, k_send, v_send, k_recv, v_recv,
-    len_send, len_recv, dk_send, dv_send, dk_recv, dv_recv, out_send, out_recv, out_sem,
+    ost, dqst, dkst, dvst, dkv, rkv, far,
+    load_sem, pair_send, pair_recv, k_send, v_send, k_recv, v_recv,
+    len_send, len_recv, grad_send, grad_recv, far_recv, out_send, out_recv, out_sem,
 ):
     prompt = lax.axis_index("prompt")
     resp = lax.axis_index("response")
@@ -72,24 +72,23 @@
 
     barrier = pltpu.get_barrier_semaphore()
 
-    @pl.loop(1, 32)
-    def _(j):
-        pl.semaphore_signal(
-            barrier,
-            inc=1,
-            device_id=at(
-                lax.rem(z + j // 8, 4),
-                lax.rem(y + lax.rem(j // 2, 4), 4),
-                lax.rem(core + lax.rem(j, 2), 2),
-            ),
-            device_id_type=MESH,
-        )
-
-    for step in range(1, 4):
-        pl.semaphore_signal(
-            barrier, inc=1, device_id=along_x(lax.rem(prompt + step, 4)), device_id_type=MESH
-        )
-    pl.semaphore_wait(barrier, 34)
+    def greet(device):
+        pl.semaphore_signal(barrier, inc=1, device_id=device, device_id_type=MESH)
+
+    for dist in (1, 3, 0):
+        for n in range(8):
+            if dist or n:
+                greet(
+                    at(
+                        lax.rem(z + dist, 4),
+                        lax.rem(y + n // 2, 4),
+                        lax.rem(core + n % 2, 2),
+                    )
+                )
+    greet(at(lax.rem(z + 2, 4), y, core))
+    for step in range(1, 4):
+        greet(along_x(lax.rem(prompt + step, 4)))
+    pl.semaphore_wait(barrier, 27)
 
     def send(src, dst, send_sem, recv_sem, device):
         return pltpu.make_async_remote_copy(
@@ -115,13 +114,13 @@
     pair[2].start()
 
     my_row = pl.multiple_of((y * 2 + core) * LOCAL, LOCAL)
-    order = ((0, 0), (1, 1), (2, 3), (3, 2))
+    up, down = lax.rem(z + 1, 4), lax.rem(z + 3, 4)
+    routes = ((0, lax.rem(z + 3 + 2 * y_hi, 4)), (1, z), (2, lax.rem(z + 5 - 2 * y_hi, 4)))
 
     def push(shard, buf, send_sems, recv_sems):
-        for block, dist in order:
-            to_z = lax.rem(z + 4 - dist, 4)
+        for block, to_z in routes:
             for n in range(8):
-                if block == 0 and n == 0:
+                if block == 1 and n == 0:
                     continue
                 to_y = lax.rem(y + n // 2, 4)
                 to_core = lax.rem(core + n % 2, 2)
@@ -129,31 +128,38 @@
                 send(
                     shard.at[:, pl.ds(cols, KCOLS)],
                     buf.at[pl.ds(block * BLOCK + my_row, LOCAL)],
-                    send_sems.at[block * 8 + n],
+                    send_sems.at[0],
                     recv_sems.at[block],
                     at(to_z, to_y, to_core),
                 ).start()
 
-    def push_done(shard, buf, send_sems, recv_sems):
-        @pl.loop(1, 32)
-        def _(n):
+    def passing(buf, send_sems, recv_sems):
+        half = BLOCK // 2
+        return [
             send(
-                shard.at[:, pl.ds(0, KCOLS)],
-                buf.at[pl.ds(0, LOCAL)],
-                send_sems.at[n],
-                recv_sems.at[0],
-                sibling,
-            ).wait_send()
+                buf.at[pl.ds(n * half, half)],
+                buf.at[pl.ds(3 * BLOCK + n * half, half)],
+                send_sems.at[1 + n],
+                recv_sems.at[3],
+                at(down if n == 0 else up, y, core),
+            )
+            for n in range(2)
+        ]
+
+    def push_done(buf, send_sems, recv_sems):
+        sent = buf.at[pl.ds(0, 23 * LOCAL)]
+        pltpu.make_async_copy(sent, sent, send_sems.at[0]).wait()
+        for copy in passing(buf, send_sems, recv_sems):
+            copy.wait_send()
 
     mine = pl.ds(pl.multiple_of((y_hi * 2 + core) * KCOLS, KCOLS), KCOLS)
     loads[0].wait()
     push(pk, kbuf, k_send, k_recv)
-    pltpu.make_async_copy(pk.at[:, mine], kbuf.at[pl.ds(my_row, LOCAL)], k_recv.at[0]).start()
+    pltpu.make_async_copy(pk.at[:, mine], kbuf.at[pl.ds(BLOCK + my_row, LOCAL)], k_recv.at[1]).start()
     pair[3].start()
     pair[4].start()
     loads[1].wait()
-    push(pv, vbuf, v_send, v_recv)
-    pltpu.make_async_copy(pv.at[:, mine], vbuf.at[pl.ds(my_row, LOCAL)], v_recv.at[0]).start()
+    pltpu.make_async_copy(pv.at[:, mine], vbuf.at[pl.ds(BLOCK + my_row, LOCAL)], v_recv.at[1]).start()
 
     def x_copy(step):
         return send(
@@ -241,6 +247,13 @@
         base = pl.multiple_of(j * BLOCK, BLOCK)
         keys = kbuf.at[pl.ds(base, BLOCK)]
         pltpu.make_async_copy(keys, keys, k_recv.at[j]).wait()
+
+        @pl.when(j == 0)
+        def _():
+            for copy in passing(kbuf, k_send, k_recv):
+                copy.start()
+            push(pv, vbuf, v_send, v_recv)
+
         for h in range(HEADS):
             cols = pl.ds(h * HD, HD)
             for n in range(BLOCK // 128):
@@ -280,6 +293,12 @@
         base = pl.multiple_of(j * BLOCK, BLOCK)
         vals = vbuf.at[pl.ds(base, BLOCK)]
         pltpu.make_async_copy(vals, vals, v_recv.at[j]).wait()
+
+        @pl.when(j == 0)
+        def _():
+            for copy in passing(vbuf, v_send, v_recv):
+                copy.start()
+
         for h in range(HEADS):
             cols = pl.ds(h * HD, HD)
             for n in range(BLOCK // 128):
@@ -307,17 +326,99 @@
         )
 
     for s in range(2):
-        live = slot_row < lsum[s, 0:1, :]
         for h in range(HEADS):
             inv = 1.0 / acc[h, s, HD : HD + 1, :]
-            attended = acc[h, s, 0:HD, :] * inv
+            acc[h, s, HD : HD + 1, :] = inv
             cotangent = dot_[h, s].astype(f32)
-            cen[h, s] = jnp.sum(attended * cotangent, axis=0, keepdims=True) * inv
+            total = jnp.sum(acc[h, s, 0:HD, :] * cotangent, axis=0, keepdims=True)
+            cen[h, s] = total * inv * inv
             scaled = (cotangent * inv).astype(bf16)
             dot_[h, s] = scaled
             for g in range(GROUP):
                 rows = slice(g * ROWS, (g + 1) * ROWS)
                 don[h, s, rows, :] = scaled[:, rows].T
+
+    half_rows = BLOCK // 2
+
+    def grad_copy(j, half, n):
+        dist = (1 - j) * (1 - 2 * half)
+        slot = (y_hi * 2 + core) * 6 + lax.rem(dist + 3, 3) * 2 + y_lo
+        row = pl.multiple_of(j * BLOCK + half * half_rows + n * LOCAL, LOCAL)
+        return send(
+            dkv.at[pl.ds(row, LOCAL)],
+            rkv.at[slot],
+            grad_send.at[0],
+            grad_recv,
+            at(lax.rem(z + dist + 4, 4), half * 2 + n // 2, n % 2),
+        )
+
+    def far_copy(half):
+        row = pl.multiple_of(3 * BLOCK + half * half_rows, half_rows)
+        return send(
+            dkv.at[pl.ds(row, half_rows)],
+            far.at[half],
+            grad_send.at[1 + half],
+            far_recv.at[half],
+            at(lax.rem(z + 1 + 2 * half, 4), y, core),
+        )
+
+    me = y * 2 + core
+
+    for h in range(HEADS):
+        for s in range(2):
+            dq[h, s] = jnp.zeros((HD, CHUNK), f32)
+
+    @pl.loop(0, 2 * NBLOCK)
+    def _(step):
+        turn = step // 2
+        j = (1 - turn // 2) * (3 - turn) + (turn // 2) * (turn - 2)
+        half = lax.rem(step + turn * (2 - turn) * (3 - turn) // 2, 2)
+        base = pl.multiple_of(j * BLOCK + half * half_rows, half_rows)
+        inner = pl.ds(pl.multiple_of(half * half_rows, half_rows), half_rows)
+        rows = pl.ds(base, half_rows)
+        for h in range(HEADS):
+            cols = pl.ds(h * HD, HD)
+            dv_part = None
+            dk_part = None
+            for s in range(2):
+                power = e[h, j, s, inner]
+                grad = dot(vbuf[rows, cols], dot_[h, s])
+                score = (power.astype(f32) * (grad - cen[h, s])).astype(bf16)
+                dv_now = dot(power, don[h, s])
+                dk_now = dot(score, qn[h, s])
+                dv_part = dv_now if s == 0 else dv_part + dv_now
+                dk_part = dk_now if s == 0 else dk_part + dk_now
+                dq[h, s] += dot(kt[h, :, pl.ds(base, half_rows)], score)
+            dkv[rows, pl.ds(h * HD, HD)] = dk_part.astype(bf16)
+            dkv[rows, pl.ds(KCOLS + h * HD, HD)] = dv_part.astype(bf16)
+
+        @pl.when(turn == 0)
+        def _():
+            far_copy(half).start()
+
+        @pl.when(turn == 2)
+        def _():
+            pltpu.make_async_copy(far.at[half], far.at[half], far_recv.at[half]).wait()
+            dkv[rows] = (dkv[rows].astype(f32) + far[half].astype(f32)).astype(bf16)
+
+        @pl.when(turn > 0)
+        def _():
+            for n in range(4):
+
+                @pl.when(jnp.logical_or(j != 1, half * 4 + n != me))
+                def _():
+                    grad_copy(j, half, n).start()
+
+    pltpu.make_async_copy(
+        dkv.at[pl.ds(BLOCK + my_row, LOCAL)], rkv.at[(y_hi * 2 + core) * 6 + y_lo], grad_recv
+    ).start()
+
+    for s in range(2):
+        live = slot_row < lsum[s, 0:1, :]
+        for h in range(HEADS):
+            attended = acc[h, s, 0:HD, :] * acc[h, s, HD : HD + 1, :]
+            for g in range(GROUP):
+                rows = slice(g * ROWS, (g + 1) * ROWS)
                 ost[s, :, pl.ds((h * GROUP + g) * HD, HD)] = jnp.where(
                     live, attended[:, rows].T, 0.0
                 ).astype(bf16)
@@ -338,59 +439,11 @@
             score = (power.astype(f32) * (grad - cen[h, s])).astype(bf16)
             dvst[s, :, cols] = (dot(power, don[h, s]) * weight).astype(bf16)
             dkst[s, :, cols] = (dot(score, qn[h, s]) * (weight * FACTOR)).astype(bf16)
-            dq[h, s] = dot(kot[h, s], score)
+            dq[h, s] += dot(kot[h, s], score)
     dk_copies = put(dkst, dk_out, my_k, 1)
     dv_copies = put(dvst, dv_out, my_k, 2)
     for copy in dk_copies + dv_copies:
         copy.start()
-
-    slot = (y_hi * 2 + core) * 8 + z * 2 + y_lo
-
-    def grad_copy(j, n, stage, landing, send_sems, recv_sem):
-        dist = j + (j // 2) * (5 - 2 * j)
-        row = pl.multiple_of(j * BLOCK + n * LOCAL, LOCAL)
-        return send(
-            stage.at[pl.ds(row, LOCAL)],
-            landing.at[slot],
-            send_sems.at[j * 8 + n],
-            recv_sem,
-            at(lax.rem(z + dist, 4), n // 2, lax.rem(n, 2)),
-        )
-
-    def self_copy(stage, landing, recv_sem):
-        return pltpu.make_async_copy(stage.at[pl.ds(my_row, LOCAL)], landing.at[slot], recv_sem)
-
-    me = y * 2 + core
-
-    @pl.loop(0, NBLOCK)
-    def _(back):
-        j = NBLOCK - 1 - back
-        base = pl.multiple_of(j * BLOCK, BLOCK)
-        for h in range(HEADS):
-            cols = pl.ds(h * HD, HD)
-            dv_part = None
-            dk_part = None
-            for s in range(2):
-                power = e[h, j, s]
-                grad = dot(vbuf[pl.ds(base, BLOCK), cols], dot_[h, s])
-                score = (power.astype(f32) * (grad - cen[h, s])).astype(bf16)
-                dv_now = dot(power, don[h, s])
-                dk_now = dot(score, qn[h, s])
-                dv_part = dv_now if s == 0 else dv_part + dv_now
-                dk_part = dk_now if s == 0 else dk_part + dk_now
-                dq[h, s] += dot(kt[h, :, pl.ds(base, BLOCK)], score)
-            dvs[pl.ds(base, BLOCK), cols] = dv_part.astype(bf16)
-            dks[pl.ds(base, BLOCK), cols] = dk_part.astype(bf16)
-
-        @pl.loop(0, 8)
-        def _(n):
-            @pl.when(jnp.logical_or(j > 0, n != me))
-            def _():
-                grad_copy(j, n, dvs, rv, dv_send, dv_recv).start()
-                grad_copy(j, n, dks, rk, dk_send, dk_recv).start()
-
-    self_copy(dvs, rv, dv_recv).start()
-    self_copy(dks, rk, dk_recv).start()
 
     for s in range(2):
         for h in range(HEADS):
@@ -403,40 +456,48 @@
     for copy in dq_copies:
         copy.start()
 
-    wide = jnp.concatenate([weight, weight], axis=1)
-    pltpu.make_async_copy(rv, rv, dv_recv).wait()
-    for n in range(4):
-        total_v = rv[n * 8].astype(f32)
-        for m in range(1, 8):
-            total_v += rv[n * 8 + m].astype(f32)
-        pvg_out[0, :, n * KCOLS : (n + 1) * KCOLS] = (total_v * wide).astype(bf16)
-    pltpu.make_async_copy(rk, rk, dk_recv).wait()
-    for n in range(4):
-        total_k = rk[n * 8].astype(f32)
-        for m in range(1, 8):
-            total_k += rk[n * 8 + m].astype(f32)
-        pkg_out[0, :, n * KCOLS : (n + 1) * KCOLS] = (total_k * (wide * FACTOR)).astype(bf16)
-
-    push_done(pk, kbuf, k_send, k_recv)
-    push_done(pv, vbuf, v_send, v_recv)
+    push_done(kbuf, k_send, k_recv)
+    push_done(vbuf, v_send, v_recv)
     for copy in pair:
         copy.wait_send()
     for step in range(1, 4):
         x_copy(step).wait_send()
         z_copy(step).wait_send()
         rest_copy(step).wait_send()
-
-    @pl.loop(0, 32)
-    def _(n):
-        @pl.when(n != me)
-        def _():
-            grad_copy(n // 8, lax.rem(n, 8), dvs, rv, dv_send, dv_recv).wait_send()
-            grad_copy(n // 8, lax.rem(n, 8), dks, rk, dk_send, dk_recv).wait_send()
-
-    for local, remote in (o_copies, dk_copies, dv_copies, dq_copies):
+    for half in range(2):
+        far_copy(half).wait_send()
+    for local, remote in (o_copies, dk_copies, dv_copies):
         local.wait()
         remote.wait_send()
         remote.wait_recv()
+    sent = dkv.at[pl.ds(0, 23 * LOCAL)]
+    pltpu.make_async_copy(sent, sent, grad_send.at[0]).wait()
+
+    pltpu.make_async_copy(rkv, rkv, grad_recv).wait()
+    twice = jnp.concatenate([weight, weight], axis=1)
+    for n in range(4):
+        summed = rkv[n * 6].astype(f32)
+        for m in range(1, 6):
+            summed += rkv[n * 6 + m].astype(f32)
+        cols = slice(n * KCOLS, (n + 1) * KCOLS)
+        pkg_out[0, :, cols] = (summed[:, :KCOLS] * (twice * FACTOR)).astype(bf16)
+        pvg_out[0, :, cols] = (summed[:, KCOLS:] * twice).astype(bf16)
+    dq_copies[0].wait()
+    dq_copies[1].wait_send()
+    dq_copies[1].wait_recv()
+
+
+def copy_kernel(*refs):
+    sources, results, held, (come, go) = refs[:6], refs[6:12], refs[12:18], refs[18:]
+    loads = [pltpu.make_async_copy(sources[n], held[n], come.at[n]) for n in range(6)]
+    stores = [pltpu.make_async_copy(held[n], results[n], go.at[n]) for n in range(6)]
+    for copy in loads:
+        copy.start()
+    for n in range(6):
+        loads[n].wait()
+        stores[n].start()
+    for copy in stores:
+        copy.wait()
 
 
 def body(queries, keys, values, prefix_keys, prefix_values, lengths, out_grad):
@@ -446,7 +507,7 @@
     anywhere = pl.BlockSpec(memory_space=pl.ANY)
     in_vmem = pl.BlockSpec(memory_space=pltpu.VMEM)
     shape = lambda a: jax.ShapeDtypeStruct(a.shape, bf16)
-    return pl.pallas_call(
+    results = pl.pallas_call(
         kernel,
         out_shape=[
             shape(queries), shape(queries), shape(keys), shape(values),
@@ -472,12 +533,13 @@
             vmem((HEADS, 2, HD, CHUNK), f32),
             vmem((2, ROWS, QCOLS), bf16), vmem((2, ROWS, QCOLS), bf16),
             vmem((2, ROWS, KCOLS), bf16), vmem((2, ROWS, KCOLS), bf16),
-            vmem((prefix, KCOLS), bf16), vmem((prefix, KCOLS), bf16),
-            vmem((32, LOCAL, KCOLS), bf16), vmem((32, LOCAL, KCOLS), bf16),
-            dma((6,)), dma((5,)), dma((5,)), dma((1,)),
-            dma((32,)), dma((32,)), dma((NBLOCK,)), dma((NBLOCK,)),
+            vmem((prefix, 2 * KCOLS), bf16),
+            vmem((24, LOCAL, 2 * KCOLS), bf16),
+            vmem((2, BLOCK // 2, 2 * KCOLS), bf16),
+            dma((6,)), dma((5,)), dma((5,)),
+            dma((3,)), dma((3,)), dma((NBLOCK,)), dma((NBLOCK,)),
             dma((3, 3)), dma((3, 3)),
-            dma((32,)), dma((32,)), dma, dma,
+            dma((3,)), dma, dma((2,)),
             dma((4,)), dma((4,)), dma((4,)),
         ],
         compiler_params=pltpu.CompilerParams(
@@ -487,6 +549,13 @@
             flops=14 * 2**30, bytes_accessed=10 * 2**20, transcendentals=9 * 2**20
         ),
     )(queries, keys, values, prefix_keys, prefix_values, lengths, out_grad)
+    return pl.pallas_call(
+        copy_kernel,
+        out_shape=[jax.ShapeDtypeStruct(a.shape, a.dtype) for a in results],
+        in_specs=[anywhere] * 6,
+        out_specs=[anywhere] * 6,
+        scratch_shapes=[vmem(a.shape, a.dtype) for a in results] + [dma((6,)), dma((6,))],
+    )(*results)
 
 
 def solution(mesh):

time: 90.7 us -> 77.7 us (0.86)
  local copies, waits for them, and re-layouts: 6.91 us -> 0 us
  Pallas kernels: 81.7 us -> 76.3 us
    pallas_call x1, Pallas kernels: 81.7 us -> 73.5 us  [body(): pl.pallas_call(kernel, out_shape=[shape(queries), shape(queries), shape(k...]
    unnamed x16 -> x0, local copies, waits for them, and re-layouts: 6.91 us -> none
    pallas_call x0 -> x1, Pallas kernels: none -> 2.81 us  [body(): pl.pallas_call(copy_kernel, out_shape=[jax.ShapeDtypeStruct(a.shape, a.dt...]
where the time goes in v2:
time: 77.7 us; the launch traced here: 77.6 us
  Pallas kernels  76.3 us (98%)
  between operations  1.29 us (2%)
    pallas_call x1, Pallas kernels, body(): pl.pallas_call(kernel, out_shape=[shape(queries), shape(queries), shape(k...  73.5 us
    pallas_call x1, Pallas kernels, body(): pl.pallas_call(copy_kernel, out_shape=[jax.ShapeDtypeStruct(a.shape, a.dt...  2.81 us

profile of v2, /device:TPU:1, one launch (start us, length us, event | category | flops | bytes accessed | tf_op | source)
XLA Modules:
  0.0 77.6 jit_solution(10962961285722276735)
XLA Ops:
  1.3 73.5 %shard_map.118 = (bf16[1,128,4096]{2,1,0:T(8,128)(2,1)}, bf16[1,128,4096]{2,1,0:T(8,128)(2,1)}, bf16[1,128,512]{2,1,0:T(8,128)(2,1)}, bf16[1,128,512]{2,1,0:T(8,...) custom-call(bf16[1,128,4096]{2,1,0:T(8,128)(2,1)} %q_in.1, bf16[1,128,512]{2,1,0:T(8,128)(2,1)} %k_in.1, ...), custom_call_target="tpu_custom_call" | custom-call | flops 15032385536 | bytes 10485760 | tf_op jit(solution)/shard_map/pallas_call | solution.py:510
  74.8 2.8 %shard_map.119 = (bf16[1,128,4096]{2,1,0:T(8,128)(2,1)}, bf16[1,128,4096]{2,1,0:T(8,128)(2,1)}, bf16[1,128,512]{2,1,0:T(8,128)(2,1)}, bf16[1,128,512]{2,1,0:T(8,...) custom-call(bf16[1,128,4096]{2,1,0:T(8,128)(2,1)} %get-tuple-element.12.refs_0_, ...), custom_call_target="tpu_custom_call" | custom-call | tf_op jit(solution)/shard_map/pallas_call | solution.py:552

commit v3 on v2

--- a/solution.py
+++ b/solution.py
@@ -113,9 +113,9 @@
     pair[1].start()
     pair[2].start()
 
-    my_row = pl.multiple_of((y * 2 + core) * LOCAL, LOCAL)
+    my_row = pl.multiple_of((core * 4 + y) * LOCAL, LOCAL)
     up, down = lax.rem(z + 1, 4), lax.rem(z + 3, 4)
-    routes = ((0, lax.rem(z + 3 + 2 * y_hi, 4)), (1, z), (2, lax.rem(z + 5 - 2 * y_hi, 4)))
+    routes = ((0, lax.rem(z + 3 + 2 * core, 4)), (1, z), (2, lax.rem(z + 5 - 2 * core, 4)))
 
     def push(shard, buf, send_sems, recv_sems):
         for block, to_z in routes:
@@ -242,6 +242,7 @@
     stage_q(1)
     own_max(1)
 
+    push(pv, vbuf, v_send, v_recv)
     @pl.loop(0, NBLOCK)
     def _(j):
         base = pl.multiple_of(j * BLOCK, BLOCK)
@@ -252,7 +253,6 @@
         def _():
             for copy in passing(kbuf, k_send, k_recv):
                 copy.start()
-            push(pv, vbuf, v_send, v_recv)
 
         for h in range(HEADS):
             cols = pl.ds(h * HD, HD)
@@ -343,13 +343,14 @@
     def grad_copy(j, half, n):
         dist = (1 - j) * (1 - 2 * half)
         slot = (y_hi * 2 + core) * 6 + lax.rem(dist + 3, 3) * 2 + y_lo
-        row = pl.multiple_of(j * BLOCK + half * half_rows + n * LOCAL, LOCAL)
+        to_y = lax.rem(y + n, 4)
+        row = pl.multiple_of(j * BLOCK + half * half_rows + to_y * LOCAL, LOCAL)
         return send(
             dkv.at[pl.ds(row, LOCAL)],
             rkv.at[slot],
             grad_send.at[0],
             grad_recv,
-            at(lax.rem(z + dist + 4, 4), half * 2 + n // 2, n % 2),
+            at(lax.rem(z + dist + 4, 4), to_y, half),
         )
 
     def far_copy(half):
@@ -362,7 +363,6 @@
             at(lax.rem(z + 1 + 2 * half, 4), y, core),
         )
 
-    me = y * 2 + core
 
     for h in range(HEADS):
         for s in range(2):
@@ -405,8 +405,12 @@
         def _():
             for n in range(4):
 
-                @pl.when(jnp.logical_or(j != 1, half * 4 + n != me))
-                def _():
+                if n == 0:
+
+                    @pl.when(jnp.logical_or(j != 1, half != core))
+                    def _():
+                        grad_copy(j, half, 0).start()
+                else:
                     grad_copy(j, half, n).start()
 
     pltpu.make_async_copy(

time: 77.7 us -> 72.4 us (0.932)
  Pallas kernels: 76.3 us -> 71 us
    pallas_call x1, Pallas kernels: 73.5 us -> 68.2 us  [body(): pl.pallas_call(kernel, out_shape=[shape(queries), shape(queries), shape(k...]
where the time goes in v3:
time: 72.4 us; the launch traced here: 72.2 us
  Pallas kernels  71 us (98%)
  between operations  1.29 us (2%)
    pallas_call x1, Pallas kernels, body(): pl.pallas_call(kernel, out_shape=[shape(queries), shape(queries), shape(k...  68.2 us
    pallas_call x1, Pallas kernels, body(): pl.pallas_call(copy_kernel, out_shape=[jax.ShapeDtypeStruct(a.shape, a.dt...  2.81 us

profile of v3, /device:TPU:1, one launch (start us, length us, event | category | flops | bytes accessed | tf_op | source)
XLA Modules:
  0.0 72.2 jit_solution(3032515818854410025)
XLA Ops:
  1.3 68.2 %shard_map.118 = (bf16[1,128,4096]{2,1,0:T(8,128)(2,1)}, bf16[1,128,4096]{2,1,0:T(8,128)(2,1)}, bf16[1,128,512]{2,1,0:T(8,128)(2,1)}, bf16[1,128,512]{2,1,0:T(8,...) custom-call(bf16[1,128,4096]{2,1,0:T(8,128)(2,1)} %q_in.1, bf16[1,128,512]{2,1,0:T(8,128)(2,1)} %k_in.1, ...), custom_call_target="tpu_custom_call" | custom-call | flops 15032385536 | bytes 10485760 | tf_op jit(solution)/shard_map/pallas_call | solution.py:514
  69.4 2.8 %shard_map.119 = (bf16[1,128,4096]{2,1,0:T(8,128)(2,1)}, bf16[1,128,4096]{2,1,0:T(8,128)(2,1)}, bf16[1,128,512]{2,1,0:T(8,128)(2,1)}, bf16[1,128,512]{2,1,0:T(8,...) custom-call(bf16[1,128,4096]{2,1,0:T(8,128)(2,1)} %get-tuple-element.12.refs_0_, ...), custom_call_target="tpu_custom_call" | custom-call | tf_op jit(solution)/shard_map/pallas_call | solution.py:556

commit v4 on v3

--- a/solution.py
+++ b/solution.py
@@ -14,7 +14,7 @@
 BLOCK = 512
 NBLOCK = 4
 CHUNK = 1024
-HALF = 512
+HALF = 1024
 HEADS = 2
 QCOLS = HEADS * GROUP * HD
 KCOLS = HEADS * HD
@@ -220,7 +220,7 @@
 
     def own_max(s):
         for h in range(HEADS):
-            for part in range(2):
+            for part in range(CHUNK // HALF):
                 cols = pl.ds(part * HALF, HALF)
                 mx[h, s, :, cols] = jnp.max(
                     own_scores(h, s, part).reshape(ROWS // 8, 8, HALF), axis=0
@@ -259,7 +259,7 @@
             for n in range(BLOCK // 128):
                 kt[h, :, pl.ds(base + n * 128, 128)] = kbuf[pl.ds(base + n * 128, 128), cols].T
             for s in range(2):
-                for part in range(2):
+                for part in range(CHUNK // HALF):
                     rows = pl.ds(part * HALF, HALF)
                     scores = dot(kbuf[pl.ds(base, BLOCK), cols], qt[h, s, :, rows])
                     mx[h, s, :, rows] = jnp.maximum(
@@ -282,7 +282,7 @@
         for s in range(2):
             top = jnp.max(mx[h, s], axis=0, keepdims=True) * EXP2
             mx[h, s] = jnp.broadcast_to(top, (8, CHUNK))
-            for part in range(2):
+            for part in range(CHUNK // HALF):
                 rows = pl.ds(part * HALF, HALF)
                 power = jnp.exp2(own_scores(h, s, part) * EXP2 - mx[h, s, 0:1, rows]).astype(bf16)
                 eo[h, s, :, rows] = power
@@ -306,7 +306,7 @@
                     pl.ds(base + n * 128, 128), cols
                 ].T
             for s in range(2):
-                for part in range(2):
+                for part in range(CHUNK // HALF):
                     rows = pl.ds(part * HALF, HALF)
                     scores = dot(kbuf[pl.ds(base, BLOCK), cols], qt[h, s, :, rows])
                     power = jnp.exp2(scores * EXP2 - mx[h, s, 0:1, rows]).astype(bf16)

time: 72.4 us -> 68.5 us (0.946)
  Pallas kernels: 71 us -> 67 us
    pallas_call x1, Pallas kernels: 68.2 us -> 64.2 us  [body(): pl.pallas_call(kernel, out_shape=[shape(queries), shape(queries), shape(k...]
where the time goes in v4:
time: 68.5 us; the launch traced here: 68.3 us
  Pallas kernels  67 us (98%)
  between operations  1.29 us (2%)
    pallas_call x1, Pallas kernels, body(): pl.pallas_call(kernel, out_shape=[shape(queries), shape(queries), shape(k...  64.2 us
    pallas_call x1, Pallas kernels, body(): pl.pallas_call(copy_kernel, out_shape=[jax.ShapeDtypeStruct(a.shape, a.dt...  2.81 us

profile of v4, /device:TPU:1, one launch (start us, length us, event | category | flops | bytes accessed | tf_op | source)
XLA Modules:
  0.0 68.3 jit_solution(12761271130407075080)
XLA Ops:
  1.3 64.2 %shard_map.118 = (bf16[1,128,4096]{2,1,0:T(8,128)(2,1)}, bf16[1,128,4096]{2,1,0:T(8,128)(2,1)}, bf16[1,128,512]{2,1,0:T(8,128)(2,1)}, bf16[1,128,512]{2,1,0:T(8,...) custom-call(bf16[1,128,4096]{2,1,0:T(8,128)(2,1)} %q_in.1, bf16[1,128,512]{2,1,0:T(8,128)(2,1)} %k_in.1, ...), custom_call_target="tpu_custom_call" | custom-call | flops 15032385536 | bytes 10485760 | tf_op jit(solution)/shard_map/pallas_call | solution.py:514
  65.5 2.8 %shard_map.119 = (bf16[1,128,4096]{2,1,0:T(8,128)(2,1)}, bf16[1,128,4096]{2,1,0:T(8,128)(2,1)}, bf16[1,128,512]{2,1,0:T(8,128)(2,1)}, bf16[1,128,512]{2,1,0:T(8,...) custom-call(bf16[1,128,4096]{2,1,0:T(8,128)(2,1)} %get-tuple-element.12.refs_0_, ...), custom_call_target="tpu_custom_call" | custom-call | tf_op jit(solution)/shard_map/pallas_call | solution.py:556

commit v5 on v4

--- a/solution.py
+++ b/solution.py
@@ -371,7 +371,8 @@
     @pl.loop(0, 2 * NBLOCK)
     def _(step):
         turn = step // 2
-        j = (1 - turn // 2) * (3 - turn) + (turn // 2) * (turn - 2)
+        middle = turn * (3 - turn) // 2
+        j = (1 - middle) * (3 - turn) + middle * (2 - lax.rem(step, 2))
         half = lax.rem(step + turn * (2 - turn) * (3 - turn) // 2, 2)
         base = pl.multiple_of(j * BLOCK + half * half_rows, half_rows)
         inner = pl.ds(pl.multiple_of(half * half_rows, half_rows), half_rows)
@@ -396,7 +397,7 @@
         def _():
             far_copy(half).start()
 
-        @pl.when(turn == 2)
+        @pl.when(turn == 3)
         def _():
             pltpu.make_async_copy(far.at[half], far.at[half], far_recv.at[half]).wait()
             dkv[rows] = (dkv[rows].astype(f32) + far[half].astype(f32)).astype(bf16)

time: 68.5 us -> 67.6 us (0.987)
  Pallas kernels: 67 us -> 66.1 us
    pallas_call x1, Pallas kernels: 64.2 us -> 63.3 us  [body(): pl.pallas_call(kernel, out_shape=[shape(queries), shape(queries), shape(k...]
where the time goes in v5:
time: 67.6 us; the launch traced here: 67.4 us
  Pallas kernels  66.1 us (98%)
  between operations  1.29 us (2%)
    pallas_call x1, Pallas kernels, body(): pl.pallas_call(kernel, out_shape=[shape(queries), shape(queries), shape(k...  63.3 us
    pallas_call x1, Pallas kernels, body(): pl.pallas_call(copy_kernel, out_shape=[jax.ShapeDtypeStruct(a.shape, a.dt...  2.81 us

profile of v5, /device:TPU:1, one launch (start us, length us, event | category | flops | bytes accessed | tf_op | source)
XLA Modules:
  0.0 67.4 jit_solution(14974731994623226034)
XLA Ops:
  1.3 63.3 %shard_map.118 = (bf16[1,128,4096]{2,1,0:T(8,128)(2,1)}, bf16[1,128,4096]{2,1,0:T(8,128)(2,1)}, bf16[1,128,512]{2,1,0:T(8,128)(2,1)}, bf16[1,128,512]{2,1,0:T(8,...) custom-call(bf16[1,128,4096]{2,1,0:T(8,128)(2,1)} %q_in.1, bf16[1,128,512]{2,1,0:T(8,128)(2,1)} %k_in.1, ...), custom_call_target="tpu_custom_call" | custom-call | flops 15032385536 | bytes 10485760 | tf_op jit(solution)/shard_map/pallas_call | solution.py:515
  64.6 2.8 %shard_map.119 = (bf16[1,128,4096]{2,1,0:T(8,128)(2,1)}, bf16[1,128,4096]{2,1,0:T(8,128)(2,1)}, bf16[1,128,512]{2,1,0:T(8,128)(2,1)}, bf16[1,128,512]{2,1,0:T(8,...) custom-call(bf16[1,128,4096]{2,1,0:T(8,128)(2,1)} %get-tuple-element.12.refs_0_, ...), custom_call_target="tpu_custom_call" | custom-call | tf_op jit(solution)/shard_map/pallas_call | solution.py:557

commit v6 on v5

--- a/solution.py
+++ b/solution.py
@@ -494,13 +494,18 @@
 
 def copy_kernel(*refs):
     sources, results, held, (come, go) = refs[:6], refs[6:12], refs[12:18], refs[18:]
-    loads = [pltpu.make_async_copy(sources[n], held[n], come.at[n]) for n in range(6)]
-    stores = [pltpu.make_async_copy(held[n], results[n], go.at[n]) for n in range(6)]
+    parts = [(n, pl.ds(32 * m, 32)) for n in (0, 1) for m in range(4)]
+    parts += [(n, slice(None)) for n in range(2, 6)]
+    loads, stores = [], []
+    for k, (n, rows) in enumerate(parts):
+        block = held[n].at[:, rows]
+        loads.append(pltpu.make_async_copy(sources[n].at[:, rows], block, come.at[k]))
+        stores.append(pltpu.make_async_copy(block, results[n].at[:, rows], go.at[k]))
     for copy in loads:
         copy.start()
-    for n in range(6):
-        loads[n].wait()
-        stores[n].start()
+    for load, store in zip(loads, stores):
+        load.wait()
+        store.start()
     for copy in stores:
         copy.wait()
 
@@ -559,7 +564,7 @@
         out_shape=[jax.ShapeDtypeStruct(a.shape, a.dtype) for a in results],
         in_specs=[anywhere] * 6,
         out_specs=[anywhere] * 6,
-        scratch_shapes=[vmem(a.shape, a.dtype) for a in results] + [dma((6,)), dma((6,))],
+        scratch_shapes=[vmem(a.shape, a.dtype) for a in results] + [dma((12,)), dma((12,))],
     )(*results)
 
 

time: 67.6 us -> 67.4 us (level)
  no operation moved by 1% of the time
where the time goes in v6:
time: 67.4 us; the launch traced here: 67.3 us
  Pallas kernels  66 us (98%)
  between operations  1.29 us (2%)
    pallas_call x1, Pallas kernels, body(): pl.pallas_call(kernel, out_shape=[shape(queries), shape(queries), shape(k...  63.3 us
    pallas_call x1, Pallas kernels, body(): pl.pallas_call(copy_kernel, out_shape=[jax.ShapeDtypeStruct(a.shape, a.dt...  2.64 us

profile of v6, /device:TPU:1, one launch (start us, length us, event | category | flops | bytes accessed | tf_op | source)
XLA Modules:
  0.0 67.3 jit_solution(10500357509343658905)
XLA Ops:
  1.3 63.3 %shard_map.118 = (bf16[1,128,4096]{2,1,0:T(8,128)(2,1)}, bf16[1,128,4096]{2,1,0:T(8,128)(2,1)}, bf16[1,128,512]{2,1,0:T(8,128)(2,1)}, bf16[1,128,512]{2,1,0:T(8,...) custom-call(bf16[1,128,4096]{2,1,0:T(8,128)(2,1)} %q_in.1, bf16[1,128,512]{2,1,0:T(8,128)(2,1)} %k_in.1, ...), custom_call_target="tpu_custom_call" | custom-call | flops 15032385536 | bytes 10485760 | tf_op jit(solution)/shard_map/pallas_call | solution.py:520
  64.6 2.6 %shard_map.119 = (bf16[1,128,4096]{2,1,0:T(8,128)(2,1)}, bf16[1,128,4096]{2,1,0:T(8,128)(2,1)}, bf16[1,128,512]{2,1,0:T(8,128)(2,1)}, bf16[1,128,512]{2,1,0:T(8,...) custom-call(bf16[1,128,4096]{2,1,0:T(8,128)(2,1)} %get-tuple-element.12.refs_0_, ...), custom_call_target="tpu_custom_call" | custom-call | tf_op jit(solution)/shard_map/pallas_call | solution.py:562
